TPU v7x, 32 devices: a whole 2x2x4 slice. The times are simulated.
32 devices in a mesh: cuts: 2 (over x), frame: 8 (over z, y), coil: 2 (over core).
Axes of the slice: x: 2, y: 2, z: 4, core: 2. Of those that a mesh axis runs over, the one named last changes fastest.
Arguments:
- spatial: bfloat16 [512, 32, 512], P(('cuts', 'coil', 'frame')), parts along dimension 0, may hold values from -6 to 6
- temporal: bfloat16 [32, 64], P(('cuts', 'frame')), parts along dimension 0, may hold values from -0.75 to 0.75
- kspace: bfloat16 [32, 32, 256, 512], P(('cuts', 'frame'), 'coil'), parts along dimension 0, may hold values from -2 to 2
- sampled: int32 [32, 256], P(('cuts', 'frame')), parts along dimension 0, may hold values 0 or 1
- sensitivity: bfloat16 [64, 256, 512], P(('cuts', 'coil')), parts along dimension 0, may hold values from -1 to 1
Outputs:
- spatial_grad: float32 [512, 32, 512], P(('cuts', 'coil', 'frame')), parts along dimension 0
- temporal_grad: float32 [32, 64], P(('cuts', 'frame')), parts along dimension 0
There are 2 independent parts, one for each index of `cuts`. A program takes and returns all parts, laid end to end along the dimension named above; each array names one. Nothing has to cross between parts.
All inputs are finite; a program needn't handle non-finite values. No bound on the sum of `sampled` on one device may be relied on, other than what follows from the above.
Results may differ from a plain program's by a relative error of at most 0.003.
Values may be sent and summed in bfloat16 or wider, within the bound.
A program may use at most 128 MiB of HBM per device.

v0:
```python
import math

import jax
import jax.numpy as jnp
from jax import lax
from jax.sharding import PartitionSpec as P


def split_parts(values):
    half_width = values.shape[-1] // 2
    return (values[..., :half_width], values[..., half_width:])


def dft_block(length):
    index = jnp.arange(length, dtype=jnp.int32)
    angles = (index[:, None] * index[None, :] % length).astype(jnp.float32) * (
        2.0 * math.pi / length
    )
    norm_factor = 1.0 / math.sqrt(length)
    cosine = jnp.cos(angles) * norm_factor
    sine_part = -jnp.sin(angles) * norm_factor
    upper_rows = jnp.concatenate([cosine, sine_part], 1)
    lower_rows = jnp.concatenate([-sine_part, cosine], 1)
    return jnp.concatenate([upper_rows, lower_rows], 0).astype(jnp.bfloat16)


def to_image(temporal, spatial):
    temp_real, temp_imag = split_parts(temporal)
    spat_real, spat_imag = split_parts(spatial)
    image_real = jnp.einsum(
        "tr,xry->txy", temp_real, spat_real, preferred_element_type=jnp.float32
    ) - jnp.einsum("tr,xry->txy", temp_imag, spat_imag, preferred_element_type=jnp.float32)
    image_imag = jnp.einsum(
        "tr,xry->txy", temp_real, spat_imag, preferred_element_type=jnp.float32
    ) + jnp.einsum("tr,xry->txy", temp_imag, spat_real, preferred_element_type=jnp.float32)
    return jnp.concatenate([image_real, image_imag], -1).astype(jnp.bfloat16)


def factor_grad(temporal, grad_image):
    temp_real, temp_imag = split_parts(temporal)
    grad_real, grad_imag = split_parts(grad_image)
    spatial_real = jnp.einsum(
        "tr,txy->xry", temp_real, grad_real, preferred_element_type=jnp.float32
    ) + jnp.einsum("tr,txy->xry", temp_imag, grad_imag, preferred_element_type=jnp.float32)
    spatial_imag = jnp.einsum(
        "tr,txy->xry", temp_real, grad_imag, preferred_element_type=jnp.float32
    ) - jnp.einsum("tr,txy->xry", temp_imag, grad_real, preferred_element_type=jnp.float32)
    return jnp.concatenate([spatial_real, spatial_imag], -1)


def frame_grad(spatial, grad_image):
    spat_real, spat_imag = split_parts(spatial)
    grad_real, grad_imag = split_parts(grad_image)
    temporal_real = jnp.einsum(
        "xry,txy->tr", spat_real, grad_real, preferred_element_type=jnp.float32
    ) + jnp.einsum("xry,txy->tr", spat_imag, grad_imag, preferred_element_type=jnp.float32)
    temporal_imag = jnp.einsum(
        "xry,txy->tr", spat_real, grad_imag, preferred_element_type=jnp.float32
    ) - jnp.einsum("xry,txy->tr", spat_imag, grad_real, preferred_element_type=jnp.float32)
    return jnp.concatenate([temporal_real, temporal_imag], -1)


def coil_adjoint(image, measured, sampled_row, sensitivity, block):
    image_real, image_imag = split_parts(image.astype(jnp.float32))
    sens_real, sens_imag = split_parts(sensitivity.astype(jnp.float32))
    coil_real = sens_real * image_real[None] - sens_imag * image_imag[None]
    coil_imag = sens_real * image_imag[None] + sens_imag * image_real[None]
    coil_image = jnp.concatenate([coil_real, coil_imag], -1).astype(jnp.bfloat16)
    coil_count, row_count, full_width = coil_image.shape
    spectrum = jnp.dot(
        coil_image.reshape(coil_count * row_count, full_width),
        block,
        preferred_element_type=jnp.float32,
    ).reshape(coil_count, row_count, full_width)
    line_keep = jnp.concatenate([sampled_row, sampled_row]).astype(jnp.float32)
    misfit = (line_keep * (spectrum - measured.astype(jnp.float32))).astype(jnp.bfloat16)
    adjoint = jnp.dot(
        misfit.reshape(coil_count * row_count, full_width),
        block.T,
        preferred_element_type=jnp.float32,
    ).reshape(coil_count, row_count, full_width)
    back_real, back_imag = split_parts(adjoint)
    grad_real = jnp.sum(sens_real * back_real + sens_imag * back_imag, axis=0)
    grad_imag = jnp.sum(sens_real * back_imag - sens_imag * back_real, axis=0)
    return jnp.concatenate([grad_real, grad_imag], -1)


def on_device(spatial, temporal, kspace, sampled, sensitivity):
    block = dft_block(spatial.shape[2] // 2)
    temporal_all = lax.all_gather(temporal, "frame", axis=0, tiled=True)
    image_rows = to_image(temporal_all, spatial)
    image_half = lax.all_to_all(image_rows, "frame", split_axis=0, concat_axis=1, tiled=True)
    image_full = lax.all_gather(image_half, "coil", axis=1, tiled=True)
    coil_partial = lax.map(
        lambda frame_item: coil_adjoint(
            frame_item[0], frame_item[1], frame_item[2], sensitivity, block
        ),
        (image_full, kspace, sampled),
    )
    grad_half = lax.psum_scatter(coil_partial, "coil", scatter_dimension=1, tiled=True).astype(
        jnp.bfloat16
    )
    grad_rows = lax.all_to_all(grad_half, "frame", split_axis=1, concat_axis=0, tiled=True)
    spatial_grad = factor_grad(temporal_all, grad_rows)
    temporal_part = lax.psum_scatter(
        frame_grad(spatial, grad_rows), "frame", scatter_dimension=0, tiled=True
    )
    temporal_grad = lax.psum(temporal_part, "coil")
    return (spatial_grad, temporal_grad)


def solution(mesh):
    placed = (
        P(("cuts", "coil", "frame"), None, None),
        P(("cuts", "frame"), None),
        P(("cuts", "frame"), "coil", None, None),
        P(("cuts", "frame"), None),
        P(("cuts", "coil"), None, None),
    )
    return jax.shard_map(
        on_device,
        mesh=mesh,
        in_specs=placed,
        out_specs=(P(("cuts", "coil", "frame"), None, None), P(("cuts", "frame"), None)),
        check_vma=False,
    )
```

profile of v0, /device:TPU:0, one launch (start us, length us, event | category | flops | bytes accessed | tf_op | source)
XLA Modules:
  0.0 152.2 jit_solution(3036720703098302424)
XLA Ops:
  0.6 22.3 %all-gather = bf16[8,2,64]{2,1,0:T(2,128)(2,1)S(1)} all-gather(bf16[1,2,64]{2,1,0:T(2,128)(2,1)} %bitcast.83), channel_id=1, replica_groups=mesh['cuts'=2,'frame'=8,'coil'=2] {'frame'}, dimensions={0}, use_global_device_ids=true | all-gather | bytes 2304 | tf_op jit(solution)/shard_map/all_gather | solution.py:90
  25.2 1.2 fusion.22
  26.4 1.2 fusion.23
  28.4 3.4 %all-to-all-start = ((bf16[16,16,512]{2,1,0:T(8,128)(2,1)}), bf16[16,16,512]{2,1,0:T(8,128)(2,1)S(1)}, u32[]{:S(2)}, u32[]{:S(2)}) async-start(bf16[16,16,512]{2,1,0:T(8,128)(2,1)} %copy.13), calls=%async_computation | async-start | bytes 524288 | tf_op jit(solution)/shard_map/all_to_all | solution.py:92
  31.9 1.3 dynamic-slice
  36.7 3.3 %all-to-all-done = bf16[16,16,512]{2,1,0:T(8,128)(2,1)S(1)} async-done(((bf16[16,16,512]{2,1,0:T(8,128)(2,1)}), bf16[16,16,512]{2,1,0:T(8,128)(2,1)S(1)}, u32[]{:S(2)}, u32[]{:S(2)}) %all-to-all-start) | async-done | bytes 262176 | tf_op jit(solution)/shard_map/all_to_all | solution.py:92
  40.0 2.2 %all_gather.7 = bf16[2,256,512]{2,1,0:T(8,128)(2,1)S(1)} all-gather(bf16[2,128,512]{2,1,0:T(8,128)(2,1)S(1)} %bitcast.70), channel_id=1, replica_groups=mesh['cuts'=2,'frame'=8,'coil'=2] {'coil'}, dimensions={1}, use_global_device_ids=true | all-gather | bytes 786432 | tf_op jit(solution)/shard_map/all_gather | solution.py:93
  42.2 62.9 %while.10 = (s32[]{:T(128)}, f32[2,256,512]{2,0,1:T(2,128)}, bf16[16,256,512]{2,1,0:T(8,128)(2,1)}, s32[2,256]{1,0:T(2,128)S(1)}, bf16[2,256,512]{2,1,0:T(8,128)...) while((s32[]{:T(128)}, f32[2,256,512]{2,0,1:T(2,128)}, ...), condition=%wide.region_3.4_spmd, body=%wide.region_0.3_spmd.sunk | while | flops 4330750976 | bytes 107749048 | solution.py:94
  42.3 3.4 %convert_element_type.64 = f32[16,256,512]{2,1,0:T(8,128)S(1)} convert(bf16[16,256,512]{2,1,0:T(8,128)(2,1)} %get-tuple-element.137) | non-fusion elementwise | flops 2097152 | bytes 12582912 | tf_op jit(solution)/shard_map/while/body/eval_jaxpr/convert_element_type | solution.py:65
  45.7 3.0 %subtract_convert_fusion.2 = (bf16[16,256,256]{2,1,0:T(8,128)(2,1)S(1)}, bf16[16,256,256]{2,1,0:T(8,128)(2,1)}) fusion(f32[16,256,512]{2,1,0:T(8,128)S(1)} %convert_element_type.64, f32[256,256]{1,0:T(8,128)S(1)} %get-tuple-element.111, f32[256,256]{1,0:T(8,128)S(1)} %get-tuple-element.112), kind=kLoop, calls=%fused_computation.13.clone.1 | loop fusion | flops 8388608 | bytes 13107200 | tf_op jit(solution)/shard_map/convert.2
  49.6 10.8 %fusion.65 = f32[16,256,512]{2,1,0:T(8,128)} fusion(bf16[2,16,256,512]{3,2,1,0:T(8,128)(2,1)} %get-tuple-element.141, s32[]{:T(128)} %get-tuple-element.126, f32[512]{0:T(512)S(1)} %add_convert_fusion.3, bf16[16,256,256]{2,1,0:T(8,128)(2,1)} %get-tuple-element.113, bf16[16,256,256]{2,1,0:T(8,128)(2,1)S(1)} %get-tuple-element.114, ...), kind=kOutput, calls=%fused_computation.3.clone.1 | convolution fusion | flops 4311744512 | bytes 17828352 | tf_op jit(solution)/shard_map/while/body/eval_jaxpr/dot_general | solution.py:77
  60.4 7.0 %add_reduce_fusion.2 = (f32[256,256]{1,0:T(8,128)S(1)}, f32[256,256]{1,0:T(8,128)S(1)}) fusion(f32[16,256,512]{2,1,0:T(8,128)} %fusion.65, f32[16,256,512]{2,1,0:T(8,128)} %copy-done), kind=kLoop, calls=%fused_computation.10.clone.1 | loop fusion | flops 8257536 | bytes 17301504 | tf_op jit(solution)/shard_map/while/body/eval_jaxpr/reduce_sum | solution.py:83
  68.0 4.7 %dynamic_update_slice.5 = f32[2,256,512]{2,0,1:T(2,128)S(1)} dynamic-update-slice(f32[2,256,512]{2,0,1:T(2,128)S(1)} %copy-done.2, f32[1,256,512]{2,0,1:T(1,128)S(1)} %copy.22, s32[]{:T(128)} %get-tuple-element.126, s32[]{:T(128)} %constant.31.clone.1..sunk, s32[]{:T(128)} %constant.31.clone.1..sunk) | dynamic-update-slice | bytes 1048580 | tf_op jit(solution)/shard_map/while/body/jit(dynamic_update_index_in_dim)/dynamic_update_slice | solution.py:94
  73.8 3.3 %convert_element_type.64 = f32[16,256,512]{2,1,0:T(8,128)S(1)} convert(bf16[16,256,512]{2,1,0:T(8,128)(2,1)} %get-tuple-element.137) | non-fusion elementwise | flops 2097152 | bytes 12582912 | tf_op jit(solution)/shard_map/while/body/eval_jaxpr/convert_element_type | solution.py:65
  77.2 3.0 %subtract_convert_fusion.2 = (bf16[16,256,256]{2,1,0:T(8,128)(2,1)S(1)}, bf16[16,256,256]{2,1,0:T(8,128)(2,1)}) fusion(f32[16,256,512]{2,1,0:T(8,128)S(1)} %convert_element_type.64, f32[256,256]{1,0:T(8,128)S(1)} %get-tuple-element.111, f32[256,256]{1,0:T(8,128)S(1)} %get-tuple-element.112), kind=kLoop, calls=%fused_computation.13.clone.1 | loop fusion | flops 8388608 | bytes 13107200 | tf_op jit(solution)/shard_map/convert.2
  81.0 10.8 %fusion.65 = f32[16,256,512]{2,1,0:T(8,128)} fusion(bf16[2,16,256,512]{3,2,1,0:T(8,128)(2,1)} %get-tuple-element.141, s32[]{:T(128)} %get-tuple-element.126, f32[512]{0:T(512)S(1)} %add_convert_fusion.3, bf16[16,256,256]{2,1,0:T(8,128)(2,1)} %get-tuple-element.113, bf16[16,256,256]{2,1,0:T(8,128)(2,1)S(1)} %get-tuple-element.114, ...), kind=kOutput, calls=%fused_computation.3.clone.1 | convolution fusion | flops 4311744512 | bytes 17828352 | tf_op jit(solution)/shard_map/while/body/eval_jaxpr/dot_general | solution.py:77
  91.8 7.0 %add_reduce_fusion.2 = (f32[256,256]{1,0:T(8,128)S(1)}, f32[256,256]{1,0:T(8,128)S(1)}) fusion(f32[16,256,512]{2,1,0:T(8,128)} %fusion.65, f32[16,256,512]{2,1,0:T(8,128)} %copy-done), kind=kLoop, calls=%fused_computation.10.clone.1 | loop fusion | flops 8257536 | bytes 17301504 | tf_op jit(solution)/shard_map/while/body/eval_jaxpr/reduce_sum | solution.py:83
  99.4 4.7 %dynamic_update_slice.5 = f32[2,256,512]{2,0,1:T(2,128)S(1)} dynamic-update-slice(f32[2,256,512]{2,0,1:T(2,128)S(1)} %copy-done.2, f32[1,256,512]{2,0,1:T(1,128)S(1)} %copy.22, s32[]{:T(128)} %get-tuple-element.126, s32[]{:T(128)} %constant.31.clone.1..sunk, s32[]{:T(128)} %constant.31.clone.1..sunk) | dynamic-update-slice | bytes 1048580 | tf_op jit(solution)/shard_map/while/body/jit(dynamic_update_index_in_dim)/dynamic_update_slice | solution.py:94
  105.1 6.9 %all-reduce.3 = bf16[2,256,512]{2,0,1:T(2,128)(2,1)S(1)} all-reduce(f32[2,256,512]{2,0,1:T(2,128)} %get-tuple-element.39), channel_id=2, replica_groups=mesh['cuts'=2,'frame'=8,'coil'=2] {'coil'}, use_global_device_ids=true, to_apply=%region_4.5.clone | all-reduce | flops 262144 | bytes 1572864
  112.9 3.4 %all-to-all-start.1 = ((bf16[2,128,512]{2,0,1:T(2,128)(2,1)}), bf16[2,128,512]{2,0,1:T(2,128)(2,1)S(1)}, u32[]{:S(2)}, u32[]{:S(2)}) async-start(bf16[2,128,512]{2,0,1:T(2,128)(2,1)} %dynamic-slice_convert_fusion), calls=%async_computation.1 | async-start | bytes 524288 | tf_op jit(solution)/shard_map/all_to_all | solution.py:103
  117.6 8.4 %all-to-all-done.1 = bf16[2,128,512]{2,0,1:T(2,128)(2,1)S(1)} async-done(((bf16[2,128,512]{2,0,1:T(2,128)(2,1)}), bf16[2,128,512]{2,0,1:T(2,128)(2,1)S(1)}, u32[]{:S(2)}, u32[]{:S(2)}) %all-to-all-start.1) | async-done | bytes 262176 | tf_op jit(solution)/shard_map/all_to_all | solution.py:103
  127.7 19.6 %all-reduce.1 = f32[16,64]{1,0:T(8,128)S(1)} all-reduce(f32[16,64]{1,0:T(8,128)S(1)} %pad_maximum_fusion.2), channel_id=3, replica_groups=mesh['cuts'=2,'frame'=8,'coil'=2] {'frame'}, use_global_device_ids=true, to_apply=%region_5.6.clone | all-reduce | flops 1024 | bytes 8192
  147.4 3.0 %psum.7 = f32[2,64]{1,0:T(2,128)} all-reduce(f32[2,64]{1,0:T(2,128)S(1)} %constant_dynamic-slice_fusion.1), channel_id=1, replica_groups=mesh['cuts'=2,'frame'=8,'coil'=2] {'coil'}, use_global_device_ids=true, to_apply=%region_6.7 | all-reduce | flops 128 | bytes 1024 | tf_op jit(solution)/shard_map/psum | solution.py:108
  151.1 1.1 pad_maximum_fusion
  (53 shorter events, 15.0 us)
Async XLA Ops:
  0.6 41.6 %copy-start.4 = (s32[2,256]{1,0:T(2,128)S(1)}, s32[2,256]{1,0:T(2,128)}, u32[]{:S(2)}) copy-start(s32[2,256]{1,0:T(2,128)} %param.10) | copy-start | bytes 6148
  28.4 11.6 %all-to-all-start = ((bf16[16,16,512]{2,1,0:T(8,128)(2,1)}), bf16[16,16,512]{2,1,0:T(8,128)(2,1)S(1)}, u32[]{:S(2)}, u32[]{:S(2)}) async-start(bf16[16,16,512]{2,1,0:T(8,128)(2,1)} %copy.13), calls=%async_computation | async-start | bytes 524288 | tf_op jit(solution)/shard_map/all_to_all | solution.py:92
  42.2 74.1 %copy-start.5 = (u32[32]{0:T(128)S(1)}, u32[32]{0:T(128)}, u32[]{:S(2)}) copy-start(u32[32]{0:T(128)} %constant.47) | copy-start | bytes 388
  42.2 84.1 %copy-start.1 = (bf16[16,32,512]{2,1,0:T(8,128)(2,1)S(1)}, bf16[16,32,512]{2,1,0:T(8,128)(2,1)}, u32[]{:S(2)}) copy-start(bf16[16,32,512]{2,1,0:T(8,128)(2,1)} %param.7) | copy-start | bytes 1572868
  45.7 3.8 %copy-start = (f32[16,256,512]{2,1,0:T(8,128)}, f32[16,256,512]{2,1,0:T(8,128)S(1)}, u32[]{:S(2)}) copy-start(f32[16,256,512]{2,1,0:T(8,128)S(1)} %convert_element_type.64) | copy-start | bytes 25165828 | tf_op jit(solution)/shard_map/while
  60.4 7.6 %copy-start.2 = (f32[2,256,512]{2,0,1:T(2,128)S(1)}, f32[2,256,512]{2,0,1:T(2,128)}, u32[]{:S(2)}) copy-start(f32[2,256,512]{2,0,1:T(2,128)} %get-tuple-element.127) | copy-start | bytes 3145732 | tf_op jit(solution)/shard_map/while
  72.7 1.0 copy-start.3
  77.2 3.8 %copy-start = (f32[16,256,512]{2,1,0:T(8,128)}, f32[16,256,512]{2,1,0:T(8,128)S(1)}, u32[]{:S(2)}) copy-start(f32[16,256,512]{2,1,0:T(8,128)S(1)} %convert_element_type.64) | copy-start | bytes 25165828 | tf_op jit(solution)/shard_map/while
  91.8 7.6 %copy-start.2 = (f32[2,256,512]{2,0,1:T(2,128)S(1)}, f32[2,256,512]{2,0,1:T(2,128)}, u32[]{:S(2)}) copy-start(f32[2,256,512]{2,0,1:T(2,128)} %get-tuple-element.127) | copy-start | bytes 3145732 | tf_op jit(solution)/shard_map/while
  104.1 1.0 copy-start.3
  112.9 13.1 %all-to-all-start.1 = ((bf16[2,128,512]{2,0,1:T(2,128)(2,1)}), bf16[2,128,512]{2,0,1:T(2,128)(2,1)S(1)}, u32[]{:S(2)}, u32[]{:S(2)}) async-start(bf16[2,128,512]{2,0,1:T(2,128)(2,1)} %dynamic-slice_convert_fusion), calls=%async_computation.1 | async-start | bytes 524288 | tf_op jit(solution)/shard_map/all_to_all | solution.py:103
where the time goes:
time: 153 us; the launch traced here: 152 us
  blocking collectives  54.1 us (35%)
  other arithmetic  31 us (20%)
  matrix products  28.1 us (18%)
  local copies, waits for them, and re-layouts  18.2 us (12%)
  waiting for transfers between devices  11.7 us (8%)
  starting transfers between devices  6.82 us (4%)
  between operations  2.1 us (1%)
    unnamed x2, blocking collectives  26.5 us
    all_gather x1, blocking collectives, on_device(): temporal_all = lax.all_gather(temporal, 'frame', axis=0, tiled=True)  22.3 us
    dot_general x2, matrix products, coil_adjoint(): jnp.dot(misfit.reshape(coil_count * row_count, full_width), block.T, pref...  21.6 us
    reduce_sum x2, other arithmetic, coil_adjoint(): grad_real = jnp.sum(sens_real * back_real + sens_imag * back_imag, axis=0)  14 us
    dynamic_update_slice x4, local copies, waits for them, and re-layouts, on_device(): lax.map(lambda frame_item: coil_adjoint(frame_item[0], frame_item[1], fra...  10.5 us
    all_to_all x1, waiting for transfers between devices, on_device(): lax.all_to_all(grad_half, 'frame', split_axis=1, concat_axis=0, tiled=True)  8.41 us
    another operation x4, other arithmetic  8 us
    convert_element_type x2, other arithmetic, coil_adjoint(): sens_real, sens_imag = split_parts(sensitivity.astype(jnp.float32))  6.72 us
  transfers between devices with their start and end apart: 2, of which 2 were waited for; matrix products, arithmetic and copies ran while one was open for 3% of the time, Pallas kernels for 0%

commit v1 on v0

v1 whole, which is shorter than its diff:
```python
import functools
import math

import jax
import jax.numpy as jnp
import ml_dtypes
import numpy as np
from jax import lax
from jax.experimental import pallas as pl
from jax.experimental.pallas import tpu as pltpu
from jax.sharding import PartitionSpec as P

BF = jnp.bfloat16
F32 = jnp.float32
MESH = pl.DeviceIdType.MESH
ROW_TILE = 16
LANES = 128


def dft_block(length):
    index = np.arange(length, dtype=np.int64)
    angles = (index[:, None] * index[None, :] % length) * (2.0 * math.pi / length)
    norm_factor = 1.0 / math.sqrt(length)
    cosine = np.cos(angles) * norm_factor
    sine_part = -np.sin(angles) * norm_factor
    block = np.block([[cosine, sine_part], [-sine_part, cosine]])
    return block.astype(np.float32).astype(ml_dtypes.bfloat16)


def mm(a, b):
    return jnp.dot(a, b, preferred_element_type=F32)


def mm_nt(a, b):
    return lax.dot_general(a, b, (((1,), (1,)), ((), ())), preferred_element_type=F32)


def xor(a, b, count):
    if count & (count - 1):
        return lax.rem(a + b, count)
    total, bit = 0, 1
    while bit < count:
        total = total + bit * lax.rem(a // bit + b // bit, 2)
        bit *= 2
    return total


def iota(shape, dim):
    return lax.broadcasted_iota(jnp.int32, shape, dim)


def one_hot(condition):
    return jnp.where(condition, 1.0, 0.0).astype(BF)


def kernel(
    dims,
    spatial_hbm, temporal_ref, kspace_hbm, sampled_ref, sens_hbm, block_hbm,
    out_hbm, tgrad_ref,
    kbuf, sbuf, spat, block, back, tslot, tall, img_send, img_recv, img_f32,
    at_real, at_imag, part_own, part_out, part_in, g_send, g_recv, g_full,
    outv, tg_send, tg_recv,
    k_sem, s_sem, spat_sem, block_sem, out_sem,
    t_ssem, t_rsem, i_ssem, i_rsem, f_ssem, f_rsem, p_ssem, p_rsem,
    g_ssem, g_rsem, tg_ssem, tg_rsem,
):
    nf, nc, frames, coils, rows, rank, width, chunk, pieces, chunks = dims
    half = width // 2
    total_frames = nf * frames
    f, c = lax.axis_index("frame"), lax.axis_index("coil")
    other = nc - 1 - c
    mine = f // pieces

    def order(step):
        if chunks < 3:
            return step
        later = (step + chunks - 1) // chunks
        return (lax.rem(step, chunks - 1) + 1) * later

    def chunk_at(step):
        return xor(mine, order(step), chunks)

    def remote(src, dst, ssem, rsem, frame, coil):
        return pltpu.make_async_remote_copy(
            src_ref=src, dst_ref=dst, send_sem=ssem, recv_sem=rsem,
            device_id={"frame": frame, "coil": coil}, device_id_type=MESH,
        )

    spat_copy = pltpu.make_async_copy(spatial_hbm, spat, spat_sem)
    block_copy = pltpu.make_async_copy(block_hbm, block, block_sem)

    def chunk_copies(step, part):
        owner = c if part == 0 else other
        start = pl.multiple_of((owner * chunks + chunk_at(step)) * chunk, chunk)
        window = pl.ds(start, chunk)
        return (
            pltpu.make_async_copy(
                kspace_hbm.at[:, :, window, :], kbuf.at[part, step], k_sem.at[part, step]
            ),
            pltpu.make_async_copy(
                sens_hbm.at[:, window, :], sbuf.at[part, step], s_sem.at[part, step]
            ),
        )

    block_copy.start()
    spat_copy.start()

    barrier = pltpu.get_barrier_semaphore()
    for shift in range(nf):
        for coil in range(nc):
            if shift or coil:
                pl.semaphore_signal(
                    barrier, inc=1,
                    device_id={"frame": xor(f, shift, nf), "coil": lax.rem(c + coil, nc)},
                    device_id_type=MESH,
                )

    @pl.loop(0, chunks)
    def _(step):
        for part in range(nc):
            for copy in chunk_copies(step, part):
                copy.start()

    tslot[f] = jnp.concatenate(
        [
            temporal_ref[...].astype(F32),
            jnp.zeros((frames, LANES - 2 * rank), F32),
        ],
        -1,
    )

    pl.semaphore_wait(barrier, nf * nc - 1)
    for shift in range(1, nf):
        to = xor(f, shift, nf)
        remote(tslot.at[f], tslot.at[f], t_ssem.at[to], t_rsem.at[f], to, c).start()

    block_copy.wait()
    cosine, sine = block[:half, :half], block[:half, half:]
    transposed = jnp.concatenate(
        [jnp.concatenate([cosine, -sine], 1), jnp.concatenate([sine, cosine], 1)], 0
    )
    diagonal = iota((width, width), 0) == iota((width, width), 1)
    for t in range(frames):
        keep = sampled_ref[t : t + 1, :].astype(F32)
        keep = jnp.concatenate([keep, keep], -1)
        selector = jnp.where(diagonal, keep, 0.0).astype(BF)
        back[t] = mm(selector, transposed).astype(BF)

    spat_copy.wait()
    for shift in range(1, nf):
        source = xor(f, shift, nf)
        remote(
            tslot.at[source], tslot.at[source], t_ssem.at[source], t_rsem.at[source], source, c
        ).wait_recv()
    for source in range(nf):
        tall[source * frames : (source + 1) * frames] = tslot[source]
    long, deep = total_frames * rows, rows * rank
    repeat = one_hot(iota((long, total_frames), 0) // rows == iota((long, total_frames), 1))
    repeated = mm(repeat, tall[...].astype(BF)).astype(BF)
    lane, column = iota((LANES, deep), 0), iota((LANES, deep), 1)
    same_row = lax.rem(iota((long, deep), 0), rows) == iota((long, deep), 1) // rank
    spread_real = one_hot(lane == lax.rem(column, rank))
    spread_imag = one_hot(lane == lax.rem(column, rank) + rank)
    a_real = jnp.where(same_row, mm(repeated, spread_real), 0.0).astype(BF)
    a_imag = jnp.where(same_row, mm(repeated, spread_imag), 0.0).astype(BF)
    factors = spat[...].reshape(deep, width)
    by_real, by_imag = mm(a_real, factors), mm(a_imag, factors)
    image = jnp.concatenate(
        [by_real[:, :half] - by_imag[:, half:], by_real[:, half:] + by_imag[:, :half]], -1
    )
    for to in range(nf):
        for t in range(frames):
            at = (to * frames + t) * rows
            img_send[to, t] = image[at : at + rows].astype(BF)
    img_recv[0, f] = img_send[f]
    for shift in range(1, nf):
        shift = shift if nf < 3 else shift % (nf - 1) + 1
        to = xor(f, shift, nf)
        remote(
            img_send.at[to], img_recv.at[0, f], i_ssem.at[to], i_rsem.at[f], to, c
        ).start()

    row, lane = iota((deep, LANES), 0), iota((deep, LANES), 1)
    same_column = iota((deep, long), 0) // rank == lax.rem(iota((deep, long), 1), rows)
    from_real = one_hot(lane == lax.rem(row, rank))
    from_imag = one_hot(lane == lax.rem(row, rank) + rank)
    at_real[...] = jnp.where(same_column, mm_nt(from_real, repeated), 0.0).astype(BF)
    at_imag[...] = jnp.where(same_column, mm_nt(from_imag, repeated), 0.0).astype(BF)

    def image_copy(source):
        return remote(
            img_send.at[source], img_recv.at[0, source], i_ssem.at[source], i_rsem.at[source],
            source, c,
        )

    def forward_copy(source):
        return remote(
            img_recv.at[0, source], img_recv.at[1, source], f_ssem.at[source],
            f_rsem.at[source], f, other,
        )

    def partial_copy(step):
        return remote(
            part_out.at[step], part_in.at[step], p_ssem.at[step], p_rsem.at[step], f, other
        )

    def gradient(step, part):
        where = chunk_at(step)
        for i in range(pieces):
            for t in range(frames):
                img_f32[t, i * rows : (i + 1) * rows] = img_recv[
                    part, where * pieces + i, t
                ].astype(F32)
        for copy in chunk_copies(step, part):
            copy.wait()
        sums = []
        for t in range(frames):
            image_real, image_imag = img_f32[t, :, :half], img_f32[t, :, half:]
            sens = sbuf[part, step].astype(F32)
            sens_real, sens_imag = sens[..., :half], sens[..., half:]
            coil_image = jnp.concatenate(
                [
                    sens_real * image_real[None] - sens_imag * image_imag[None],
                    sens_real * image_imag[None] + sens_imag * image_real[None],
                ],
                -1,
            ).astype(BF)
            spectrum = mm(coil_image.reshape(coils * chunk, width), block[...])
            measured = kbuf[part, step, t].reshape(coils * chunk, width).astype(F32)
            misfit = (spectrum - measured).astype(BF)
            adjoint = mm(misfit, back[t]).reshape(coils, chunk, width)
            back_real, back_imag = adjoint[..., :half], adjoint[..., half:]
            sums.append(
                jnp.concatenate(
                    [
                        jnp.sum(sens_real * back_real + sens_imag * back_imag, axis=0),
                        jnp.sum(sens_real * back_imag - sens_imag * back_real, axis=0),
                    ],
                    -1,
                )
            )
        return sums

    def finish(step):
        where = chunk_at(step)
        partial_copy(step).wait_recv()
        for t in range(frames):
            total = part_own[step, t] + part_in[step, t]
            for i in range(pieces):
                g_send[where * pieces + i, t] = total[i * rows : (i + 1) * rows].astype(BF)
        for i in range(pieces):
            to = where * pieces + i

            @pl.when(to != f)
            def _():
                remote(
                    g_send.at[to], g_recv.at[f], g_ssem.at[to], g_rsem.at[f], to, c
                ).start()

            @pl.when(to == f)
            def _():
                g_recv[f] = g_send[f]

    @pl.loop(0, chunks)
    def _(step):
        where = chunk_at(step)
        for i in range(pieces):
            source = where * pieces + i

            @pl.when(source != f)
            def _():
                image_copy(source).wait_recv()

            forward_copy(source).start()
        for t, value in enumerate(gradient(step, 0)):
            part_own[step, t] = value

        @pl.when(step > 0)
        def _():
            finish(step - 1)

        for i in range(pieces):
            forward_copy(where * pieces + i).wait_recv()
        for t, value in enumerate(gradient(step, 1)):
            part_out[step, t] = value
        partial_copy(step).start()

    finish(chunks - 1)

    def gradient_copy(source):
        return remote(
            g_send.at[source], g_recv.at[source], g_ssem.at[source], g_rsem.at[source], source, c
        )

    for shift in range(1, nf):
        gradient_copy(xor(f, shift, nf)).wait_recv()
    for source in range(nf):
        for t in range(frames):
            at = (source * frames + t) * rows
            g_full[at : at + rows] = g_recv[source, t].astype(F32)
    grad = g_full[...].astype(BF)
    turned = jnp.concatenate([grad[:, half:], -grad[:, :half]], -1)
    factors = spat[...].reshape(deep, width)
    fold_row, fold_lane = iota((deep, LANES), 0), iota((deep, LANES), 1)
    pooled = jnp.zeros((long, LANES), F32)
    for values, shift in ((grad, 0), (turned, rank)):
        products = jnp.where(same_row, mm_nt(values, factors), 0.0)
        fold = one_hot(lax.rem(fold_row, rank) + shift == fold_lane)
        high = products.astype(BF)
        low = (products - high.astype(F32)).astype(BF)
        pooled = pooled + mm(high, fold) + mm(low, fold)
    gather = one_hot(iota((total_frames, long), 0) == iota((total_frames, long), 1) // rows)
    high = pooled.astype(BF)
    low = (pooled - high.astype(F32)).astype(BF)
    temporal_part = mm(gather, high) + mm(gather, low)
    for to in range(nf):
        tg_send[to] = temporal_part[to * frames : (to + 1) * frames]
    tg_recv[c, f] = tg_send[f]
    for shift in range(nf):
        for coil in range(nc):
            if shift or coil:
                to, at = xor(f, shift, nf), lax.rem(c + coil, nc)
                remote(
                    tg_send.at[to], tg_recv.at[c, f], tg_ssem.at[at, to], tg_rsem.at[c, f], to, at
                ).start()

    by_real, by_imag = mm(at_real[...], grad), mm(at_imag[...], grad)
    outv[...] = jnp.concatenate(
        [by_real[:, :half] + by_imag[:, half:], by_real[:, half:] - by_imag[:, :half]], -1
    ).reshape(rows, rank, width)
    out_copy = pltpu.make_async_copy(outv, out_hbm, out_sem)
    out_copy.start()

    for shift in range(nf):
        for coil in range(nc):
            if shift or coil:
                to, at = xor(f, shift, nf), lax.rem(c + coil, nc)
                remote(
                    tg_send.at[to], tg_recv.at[at, to], tg_ssem.at[at, to], tg_rsem.at[at, to],
                    to, at,
                ).wait()
    summed = tg_recv[0, 0]
    for coil in range(nc):
        for source in range(nf):
            if coil or source:
                summed = summed + tg_recv[coil, source]
    tgrad_ref[...] = summed[:, : 2 * rank]

    for shift in range(nf):
        to = xor(f, shift, nf)
        forward_copy(to).wait_send()
        if shift:
            remote(tslot.at[f], tslot.at[f], t_ssem.at[to], t_rsem.at[f], to, c).wait_send()
            image_copy(to).wait_send()
            gradient_copy(to).wait_send()

    @pl.loop(0, chunks)
    def _(step):
        partial_copy(step).wait_send()

    out_copy.wait()


def on_device(nf, nc, spatial, temporal, kspace, sampled, sensitivity):
    rows, rank, width = spatial.shape
    frames, coils = kspace.shape[:2]
    chunk = max(rows, ROW_TILE)
    pieces = chunk // rows
    chunks = nf // pieces
    total_frames = nf * frames
    long, deep = total_frames * rows, rows * rank
    dims = (nf, nc, frames, coils, rows, rank, width, chunk, pieces, chunks)
    vmem, dma = pltpu.VMEM, pltpu.SemaphoreType.DMA
    anywhere, inside = pl.BlockSpec(memory_space=pl.ANY), pl.BlockSpec(memory_space=pltpu.VMEM)
    return pl.pallas_call(
        functools.partial(kernel, dims),
        out_shape=(
            jax.ShapeDtypeStruct(spatial.shape, F32),
            jax.ShapeDtypeStruct(temporal.shape, F32),
        ),
        in_specs=[anywhere, inside, anywhere, inside, anywhere, anywhere],
        out_specs=(anywhere, inside),
        scratch_shapes=[
            vmem((nc, chunks, frames, coils, chunk, width), BF),
            vmem((nc, chunks, coils, chunk, width), BF),
            vmem((rows, rank, width), BF),
            vmem((width, width), BF),
            vmem((frames, width, width), BF),
            vmem((nf, frames, LANES), F32),
            vmem((total_frames, LANES), F32),
            vmem((nf, frames, rows, width), BF),
            vmem((nc, nf, frames, rows, width), BF),
            vmem((frames, chunk, width), F32),
            vmem((deep, long), BF),
            vmem((deep, long), BF),
            vmem((chunks, frames, chunk, width), F32),
            vmem((chunks, frames, chunk, width), F32),
            vmem((chunks, frames, chunk, width), F32),
            vmem((nf, frames, rows, width), BF),
            vmem((nf, frames, rows, width), BF),
            vmem((long, width), F32),
            vmem((rows, rank, width), F32),
            vmem((nf, frames, LANES), F32),
            vmem((nc, nf, frames, LANES), F32),
            dma((nc, chunks)),
            dma((nc, chunks)),
            dma,
            dma,
            dma,
        ]
        + [dma((nf,))] * 6
        + [dma((chunks,))] * 2
        + [dma((nf,))] * 2
        + [dma((nc, nf))] * 2,
        compiler_params=pltpu.CompilerParams(
            collective_id=0, has_side_effects=True, vmem_limit_bytes=56 * 1024 * 1024
        ),
        cost_estimate=pl.CostEstimate(
            flops=8 * frames * coils * nc * chunks * chunk * width * width // 2,
            bytes_accessed=kspace.size * 2 + sensitivity.size * 2 + spatial.size * 6,
            transcendentals=0,
        ),
    )(spatial, temporal, kspace, sampled, sensitivity, jnp.asarray(dft_block(width // 2)))


def solution(mesh):
    placed = (
        P(("cuts", "coil", "frame"), None, None),
        P(("cuts", "frame"), None),
        P(("cuts", "frame"), "coil", None, None),
        P(("cuts", "frame"), None),
        P(("cuts", "coil"), None, None),
    )
    return jax.shard_map(
        functools.partial(on_device, mesh.shape["frame"], mesh.shape["coil"]),
        mesh=mesh,
        in_specs=placed,
        out_specs=(P(("cuts", "coil", "frame"), None, None), P(("cuts", "frame"), None)),
        check_vma=False,
    )
```

time: 153 us -> 42.7 us (0.28)
  blocking collectives: 54.1 us -> 0 us
  Pallas kernels: 0 us -> 38.4 us
  other arithmetic: 31 us -> 0 us
  matrix products: 28.1 us -> 0 us
  local copies, waits for them, and re-layouts: 18.2 us -> 3.53 us
  waiting for transfers between devices: 11.7 us -> 0 us
  starting transfers between devices: 6.82 us -> 0 us
    pallas_call x0 -> x1, Pallas kernels: none -> 38.4 us  [on_device(): pl.pallas_call(functools.partial(kernel, dims), out_shape=(jax.ShapeDtype...]
    dot_general x14 -> x0, matrix products: 28.1 us -> none  [the longest x2 21.6 us: coil_adjoint(): jnp.dot(misfit.reshape(coil_count * row_count, full_width), block.T, pref...]
    unnamed x2 -> x0, blocking collectives: 26.5 us -> none
    all_gather x2 -> x0, blocking collectives: 24.5 us -> none  [the longest x1 22.3 us: on_device(): temporal_all = lax.all_gather(temporal, 'frame', axis=0, tiled=True)]
    reduce_sum x2 -> x0, other arithmetic: 14 us -> none  [coil_adjoint(): grad_real = jnp.sum(sens_real * back_real + sens_imag * back_imag, axis=0)]
    all_to_all x2 -> x0, waiting for transfers between devices: 11.7 us -> none  [the longest x1 8.41 us: on_device(): lax.all_to_all(grad_half, 'frame', split_axis=1, concat_axis=0, tiled=True)]
    dynamic_update_slice x4 -> x0, local copies, waits for them, and re-layouts: 10.5 us -> none  [on_device(): lax.map(lambda frame_item: coil_adjoint(frame_item[0], frame_item[1], fra...]
    another operation x4 -> x0, other arithmetic: 8 us -> none
  transfers between devices with their start and end apart: 2 -> 0, of which waited for: 2 -> 0; matrix products, arithmetic and copies ran while one was open for 3% -> 0% of each run, Pallas kernels for 0% -> 0%
where the time goes in v1:
time: 42.7 us; the launch traced here: 42.5 us
  Pallas kernels  38.4 us (90%)
  local copies, waits for them, and re-layouts  3.53 us (8%)
  between operations  0.64 us (1%)
    pallas_call x1, Pallas kernels, on_device(): pl.pallas_call(functools.partial(kernel, dims), out_shape=(jax.ShapeDtype...  38.4 us
    unnamed x2, local copies, waits for them, and re-layouts  3.53 us

profile of v1, /device:TPU:0, one launch (start us, length us, event | category | flops | bytes accessed | tf_op | source)
XLA Modules:
  0.0 42.5 jit_solution(12625503350454960801)
XLA Ops:
  0.6 38.4 %shard_map.77 = (f32[16,32,512]{2,1,0:T(8,128)}, f32[2,64]{1,0:T(2,128)}) custom-call(bf16[16,32,512]{2,1,0:T(8,128)(2,1)} %spatial_hbm.1, bf16[2,64]{1,0:T(2,128)(2,1)} %temporal_ref.1, bf16[2,16,256,512]{3,2,1,0:T(8,128)(2,1)} %kspace_hbm.1, s32[2,256]{1,0:T(2,128)} %sampled_ref.1, bf16[16,256,512]{2,1,0:T(8,128)(2,1)} %sens_hbm.1, ...), custom_call_target="tpu_custom_call" | custom-call | flops 8589934592 | bytes 14155776 | tf_op jit(solution)/shard_map/pallas_call | solution.py:375
  39.0 2.3 %copy.10 = f32[16,32,512]{2,1,0:T(8,128)} copy(f32[16,32,512]{2,1,0:T(8,128)} %get-tuple-element.4) | data formatting | bytes 2097152
  41.3 1.2 %copy.11 = f32[2,64]{1,0:T(2,128)} copy(f32[2,64]{1,0:T(2,128)} %get-tuple-element.5) | data formatting | bytes 1024

commit v2 on v1

--- a/solution.py
+++ b/solution.py
@@ -57,7 +57,7 @@
     dims,
     spatial_hbm, temporal_ref, kspace_hbm, sampled_ref, sens_hbm, block_hbm,
     out_hbm, tgrad_ref,
-    kbuf, sbuf, spat, block, back, tslot, tall, img_send, img_recv, img_f32,
+    kbuf, sbuf, spat, block, back, keep, ci0, ci1, mis0, mis1, tslot, tall, img_send, img_recv, img_f32,
     at_real, at_imag, part_own, part_out, part_in, g_send, g_recv, g_full,
     outv, tg_send, tg_recv,
     k_sem, s_sem, spat_sem, block_sem, out_sem,
@@ -136,15 +136,13 @@
 
     block_copy.wait()
     cosine, sine = block[:half, :half], block[:half, half:]
-    transposed = jnp.concatenate(
-        [jnp.concatenate([cosine, -sine], 1), jnp.concatenate([sine, cosine], 1)], 0
-    )
-    diagonal = iota((width, width), 0) == iota((width, width), 1)
+    back[:half] = jnp.concatenate([cosine, -sine], 1)
+    back[half:] = jnp.concatenate([sine, cosine], 1)
     for t in range(frames):
-        keep = sampled_ref[t : t + 1, :].astype(F32)
-        keep = jnp.concatenate([keep, keep], -1)
-        selector = jnp.where(diagonal, keep, 0.0).astype(BF)
-        back[t] = mm(selector, transposed).astype(BF)
+        lines = sampled_ref[t : t + 1, :].astype(F32)
+        lines = jnp.concatenate([lines, lines], -1)
+        keep[t] = jnp.broadcast_to(lines, (chunk, width)).astype(BF)
+    mis1[...] = jnp.zeros_like(mis1)
 
     spat_copy.wait()
     for shift in range(1, nf):
@@ -201,45 +199,50 @@
 
     def partial_copy(step):
         return remote(
-            part_out.at[step], part_in.at[step], p_ssem.at[step], p_rsem.at[step], f, other
-        )
-
-    def gradient(step, part):
-        where = chunk_at(step)
-        for i in range(pieces):
-            for t in range(frames):
-                img_f32[t, i * rows : (i + 1) * rows] = img_recv[
-                    part, where * pieces + i, t
-                ].astype(F32)
+            part_out.at[step + 1], part_in.at[step], p_ssem.at[step], p_rsem.at[step], f, other
+        )
+
+    tile = (frames, coils, chunk, width)
+
+    def await_chunk(step, part):
         for copy in chunk_copies(step, part):
             copy.wait()
-        sums = []
-        for t in range(frames):
-            image_real, image_imag = img_f32[t, :, :half], img_f32[t, :, half:]
-            sens = sbuf[part, step].astype(F32)
-            sens_real, sens_imag = sens[..., :half], sens[..., half:]
-            coil_image = jnp.concatenate(
-                [
-                    sens_real * image_real[None] - sens_imag * image_imag[None],
-                    sens_real * image_imag[None] + sens_imag * image_real[None],
-                ],
-                -1,
-            ).astype(BF)
-            spectrum = mm(coil_image.reshape(coils * chunk, width), block[...])
-            measured = kbuf[part, step, t].reshape(coils * chunk, width).astype(F32)
-            misfit = (spectrum - measured).astype(BF)
-            adjoint = mm(misfit, back[t]).reshape(coils, chunk, width)
-            back_real, back_imag = adjoint[..., :half], adjoint[..., half:]
-            sums.append(
-                jnp.concatenate(
-                    [
-                        jnp.sum(sens_real * back_real + sens_imag * back_imag, axis=0),
-                        jnp.sum(sens_real * back_imag - sens_imag * back_real, axis=0),
-                    ],
-                    -1,
-                )
-            )
-        return sums
+
+    def coil_images(step, part, out):
+        where = chunk_at(step)
+        sens = sbuf[part, step].astype(F32)
+        sens_real, sens_imag = sens[..., :half], sens[..., half:]
+        size = coils * chunk
+        for t in range(frames):
+            if pieces == 1:
+                image = img_recv[part, where, t].astype(F32)
+            else:
+                for i in range(pieces):
+                    img_f32[part, t, i * rows : (i + 1) * rows] = img_recv[
+                        part, where * pieces + i, t
+                    ].astype(F32)
+                image = img_f32[part, t]
+            image_real, image_imag = image[:, :half], image[:, half:]
+            real = sens_real * image_real[None] - sens_imag * image_imag[None]
+            imag = sens_real * image_imag[None] + sens_imag * image_real[None]
+            out[t * size : (t + 1) * size, :half] = real.astype(BF).reshape(size, half)
+            out[t * size : (t + 1) * size, half:] = imag.astype(BF).reshape(size, half)
+
+    def misfits(step, part, source, out):
+        spectrum = mm(source[...], block[...]).reshape(tile)
+        for t in range(frames):
+            misfit = (spectrum[t] - kbuf[part, step, t].astype(F32)).astype(BF) * keep[t][None]
+            size = coils * chunk
+            out[t * size : (t + 1) * size] = misfit.reshape(size, width)
+
+    def coil_sums(step, part, source, out, slot):
+        adjoint = mm(source[...], back[...]).reshape(tile)
+        sens = sbuf[part, step].astype(F32)
+        sens_real, sens_imag = sens[..., :half], sens[..., half:]
+        for t in range(frames):
+            back_real, back_imag = adjoint[t, ..., :half], adjoint[t, ..., half:]
+            out[slot, t, :, :half] = jnp.sum(sens_real * back_real + sens_imag * back_imag, axis=0)
+            out[slot, t, :, half:] = jnp.sum(sens_real * back_imag - sens_imag * back_real, axis=0)
 
     def finish(step):
         where = chunk_at(step)
@@ -261,30 +264,54 @@
             def _():
                 g_recv[f] = g_send[f]
 
+    def forward(step):
+        where = chunk_at(step)
+        for i in range(pieces):
+            source = where * pieces + i
+
+            @pl.when(source != f)
+            def _():
+                image_copy(source).wait_recv()
+
+            forward_copy(source).start()
+
+    forward(0)
+    await_chunk(0, 0)
+    coil_images(0, 0, ci0)
+
     @pl.loop(0, chunks)
     def _(step):
         where = chunk_at(step)
+        before = jnp.maximum(step - 1, 0)
+        after = jnp.minimum(step + 1, chunks - 1)
         for i in range(pieces):
-            source = where * pieces + i
-
-            @pl.when(source != f)
-            def _():
-                image_copy(source).wait_recv()
-
-            forward_copy(source).start()
-        for t, value in enumerate(gradient(step, 0)):
-            part_own[step, t] = value
+            forward_copy(where * pieces + i).wait_recv()
+        await_chunk(step, 1)
+        coil_sums(before, 1, mis1, part_out, step)
+        misfits(step, 0, ci0, mis0)
+        coil_images(step, 1, ci1)
 
         @pl.when(step > 0)
         def _():
-            finish(step - 1)
-
-        for i in range(pieces):
-            forward_copy(where * pieces + i).wait_recv()
-        for t, value in enumerate(gradient(step, 1)):
-            part_out[step, t] = value
-        partial_copy(step).start()
-
+            partial_copy(step - 1).start()
+
+        @pl.when(step > 1)
+        def _():
+            finish(step - 2)
+
+        @pl.when(step < chunks - 1)
+        def _():
+            forward(step + 1)
+            await_chunk(step + 1, 0)
+
+        coil_sums(step, 0, mis0, part_own, step)
+        misfits(step, 1, ci1, mis1)
+        coil_images(after, 0, ci0)
+
+    coil_sums(chunks - 1, 1, mis1, part_out, chunks)
+    partial_copy(chunks - 1).start()
+    if chunks > 1:
+        finish(chunks - 2)
     finish(chunks - 1)
 
     def gradient_copy(source):
@@ -371,30 +398,34 @@
     long, deep = total_frames * rows, rows * rank
     dims = (nf, nc, frames, coils, rows, rank, width, chunk, pieces, chunks)
     vmem, dma = pltpu.VMEM, pltpu.SemaphoreType.DMA
-    anywhere, inside = pl.BlockSpec(memory_space=pl.ANY), pl.BlockSpec(memory_space=pltpu.VMEM)
+    outside, inside = pl.BlockSpec(memory_space=pl.ANY), pl.BlockSpec(memory_space=pltpu.VMEM)
     return pl.pallas_call(
         functools.partial(kernel, dims),
         out_shape=(
             jax.ShapeDtypeStruct(spatial.shape, F32),
             jax.ShapeDtypeStruct(temporal.shape, F32),
         ),
-        in_specs=[anywhere, inside, anywhere, inside, anywhere, anywhere],
-        out_specs=(anywhere, inside),
+        in_specs=[outside, inside, outside, inside, outside, outside],
+        out_specs=(outside, inside),
         scratch_shapes=[
             vmem((nc, chunks, frames, coils, chunk, width), BF),
             vmem((nc, chunks, coils, chunk, width), BF),
             vmem((rows, rank, width), BF),
             vmem((width, width), BF),
-            vmem((frames, width, width), BF),
+            vmem((width, width), BF),
+            vmem((frames, chunk, width), BF),
+        ]
+        + [vmem((frames * coils * chunk, width), BF)] * 4
+        + [
             vmem((nf, frames, LANES), F32),
             vmem((total_frames, LANES), F32),
             vmem((nf, frames, rows, width), BF),
             vmem((nc, nf, frames, rows, width), BF),
-            vmem((frames, chunk, width), F32),
+            vmem((nc, frames, chunk, width), F32),
             vmem((deep, long), BF),
             vmem((deep, long), BF),
             vmem((chunks, frames, chunk, width), F32),
-            vmem((chunks, frames, chunk, width), F32),
+            vmem((chunks + 1, frames, chunk, width), F32),
             vmem((chunks, frames, chunk, width), F32),
             vmem((nf, frames, rows, width), BF),
             vmem((nf, frames, rows, width), BF),
@@ -413,7 +444,7 @@
         + [dma((nf,))] * 2
         + [dma((nc, nf))] * 2,
         compiler_params=pltpu.CompilerParams(
-            collective_id=0, has_side_effects=True, vmem_limit_bytes=56 * 1024 * 1024
+            collective_id=0, has_side_effects=True, vmem_limit_bytes=61 * 1024 * 1024
         ),
         cost_estimate=pl.CostEstimate(
             flops=8 * frames * coils * nc * chunks * chunk * width * width // 2,

time: 42.7 us -> 44.4 us (1.040)
  Pallas kernels: 38.4 us -> 40.1 us
    pallas_call x1, Pallas kernels: 38.4 us -> 40.1 us  [on_device(): pl.pallas_call(functools.partial(kernel, dims), out_shape=(jax.ShapeDtype...]
where the time goes in v2:
time: 44.4 us; the launch traced here: 44.2 us
  Pallas kernels  40.1 us (90%)
  local copies, waits for them, and re-layouts  3.53 us (8%)
  between operations  0.64 us (1%)
    pallas_call x1, Pallas kernels, on_device(): pl.pallas_call(functools.partial(kernel, dims), out_shape=(jax.ShapeDtype...  40.1 us
    unnamed x2, local copies, waits for them, and re-layouts  3.53 us

profile of v2, /device:TPU:0, one launch (start us, length us, event | category | flops | bytes accessed | tf_op | source)
XLA Modules:
  0.0 44.2 jit_solution(9188335553596507507)
XLA Ops:
  0.6 40.1 %shard_map.77 = (f32[16,32,512]{2,1,0:T(8,128)}, f32[2,64]{1,0:T(2,128)}) custom-call(bf16[16,32,512]{2,1,0:T(8,128)(2,1)} %spatial_hbm.1, bf16[2,64]{1,0:T(2,128)(2,1)} %temporal_ref.1, bf16[2,16,256,512]{3,2,1,0:T(8,128)(2,1)} %kspace_hbm.1, s32[2,256]{1,0:T(2,128)} %sampled_ref.1, bf16[16,256,512]{2,1,0:T(8,128)(2,1)} %sens_hbm.1, ...), custom_call_target="tpu_custom_call" | custom-call | flops 8589934592 | bytes 14155776 | tf_op jit(solution)/shard_map/pallas_call | solution.py:402
  40.7 2.3 %copy.10 = f32[16,32,512]{2,1,0:T(8,128)} copy(f32[16,32,512]{2,1,0:T(8,128)} %get-tuple-element.4) | data formatting | bytes 2097152
  43.0 1.2 %copy.11 = f32[2,64]{1,0:T(2,128)} copy(f32[2,64]{1,0:T(2,128)} %get-tuple-element.5) | data formatting | bytes 1024

commit v3 on v1

--- a/solution.py
+++ b/solution.py
@@ -14,6 +14,7 @@
 F32 = jnp.float32
 MESH = pl.DeviceIdType.MESH
 ROW_TILE = 16
+AHEAD = 3
 LANES = 128
 
 
@@ -56,11 +57,11 @@
 def kernel(
     dims,
     spatial_hbm, temporal_ref, kspace_hbm, sampled_ref, sens_hbm, block_hbm,
-    out_hbm, tgrad_ref,
+    turn_hbm, grad_hbm, tgrad_ref,
     kbuf, sbuf, spat, block, back, tslot, tall, img_send, img_recv, img_f32,
-    at_real, at_imag, part_own, part_out, part_in, g_send, g_recv, g_full,
-    outv, tg_send, tg_recv,
-    k_sem, s_sem, spat_sem, block_sem, out_sem,
+    turn, part_own, part_out, part_in, g_send, g_recv, g_full,
+    grad_rows, tg_send, tg_recv,
+    k_sem, s_sem, spat_sem, block_sem, turn_sem, grad_sem,
     t_ssem, t_rsem, i_ssem, i_rsem, f_ssem, f_rsem, p_ssem, p_rsem,
     g_ssem, g_rsem, tg_ssem, tg_rsem,
 ):
@@ -115,12 +116,12 @@
                     device_id_type=MESH,
                 )
 
-    @pl.loop(0, chunks)
-    def _(step):
+    def fetch(step):
         for part in range(nc):
             for copy in chunk_copies(step, part):
                 copy.start()
 
+    fetch(0)
     tslot[f] = jnp.concatenate(
         [
             temporal_ref[...].astype(F32),
@@ -180,12 +181,17 @@
             img_send.at[to], img_recv.at[0, f], i_ssem.at[to], i_rsem.at[f], to, c
         ).start()
 
+    for step in range(1, min(AHEAD, chunks)):
+        fetch(step)
+
     row, lane = iota((deep, LANES), 0), iota((deep, LANES), 1)
     same_column = iota((deep, long), 0) // rank == lax.rem(iota((deep, long), 1), rows)
     from_real = one_hot(lane == lax.rem(row, rank))
     from_imag = one_hot(lane == lax.rem(row, rank) + rank)
-    at_real[...] = jnp.where(same_column, mm_nt(from_real, repeated), 0.0).astype(BF)
-    at_imag[...] = jnp.where(same_column, mm_nt(from_imag, repeated), 0.0).astype(BF)
+    turn[:, :long] = jnp.where(same_column, mm_nt(from_real, repeated), 0.0).astype(BF)
+    turn[:, long:] = jnp.where(same_column, mm_nt(from_imag, repeated), 0.0).astype(BF)
+    turn_copy = pltpu.make_async_copy(turn, turn_hbm, turn_sem)
+    turn_copy.start()
 
     def image_copy(source):
         return remote(
@@ -263,6 +269,10 @@
 
     @pl.loop(0, chunks)
     def _(step):
+        @pl.when(step + AHEAD < chunks)
+        def _():
+            fetch(step + AHEAD)
+
         where = chunk_at(step)
         for i in range(pieces):
             source = where * pieces + i
@@ -300,6 +310,10 @@
             g_full[at : at + rows] = g_recv[source, t].astype(F32)
     grad = g_full[...].astype(BF)
     turned = jnp.concatenate([grad[:, half:], -grad[:, :half]], -1)
+    grad_rows[:long] = grad
+    grad_rows[long:] = turned
+    grad_copy = pltpu.make_async_copy(grad_rows, grad_hbm, grad_sem)
+    grad_copy.start()
     factors = spat[...].reshape(deep, width)
     fold_row, fold_lane = iota((deep, LANES), 0), iota((deep, LANES), 1)
     pooled = jnp.zeros((long, LANES), F32)
@@ -324,13 +338,6 @@
                     tg_send.at[to], tg_recv.at[c, f], tg_ssem.at[at, to], tg_rsem.at[c, f], to, at
                 ).start()
 
-    by_real, by_imag = mm(at_real[...], grad), mm(at_imag[...], grad)
-    outv[...] = jnp.concatenate(
-        [by_real[:, :half] + by_imag[:, half:], by_real[:, half:] - by_imag[:, :half]], -1
-    ).reshape(rows, rank, width)
-    out_copy = pltpu.make_async_copy(outv, out_hbm, out_sem)
-    out_copy.start()
-
     for shift in range(nf):
         for coil in range(nc):
             if shift or coil:
@@ -358,7 +365,13 @@
     def _(step):
         partial_copy(step).wait_send()
 
-    out_copy.wait()
+    turn_copy.wait()
+    grad_copy.wait()
+
+
+def factor_kernel(turn_ref, grad_ref, tsum_ref, out_ref, tgrad_ref):
+    out_ref[...] = mm(turn_ref[...], grad_ref[...]).reshape(out_ref.shape)
+    tgrad_ref[...] = tsum_ref[...]
 
 
 def on_device(nf, nc, spatial, temporal, kspace, sampled, sensitivity):
@@ -372,14 +385,15 @@
     dims = (nf, nc, frames, coils, rows, rank, width, chunk, pieces, chunks)
     vmem, dma = pltpu.VMEM, pltpu.SemaphoreType.DMA
     anywhere, inside = pl.BlockSpec(memory_space=pl.ANY), pl.BlockSpec(memory_space=pltpu.VMEM)
-    return pl.pallas_call(
+    turn, grad_rows, temporal_sum = pl.pallas_call(
         functools.partial(kernel, dims),
         out_shape=(
-            jax.ShapeDtypeStruct(spatial.shape, F32),
+            jax.ShapeDtypeStruct((deep, 2 * long), BF),
+            jax.ShapeDtypeStruct((2 * long, width), BF),
             jax.ShapeDtypeStruct(temporal.shape, F32),
         ),
         in_specs=[anywhere, inside, anywhere, inside, anywhere, anywhere],
-        out_specs=(anywhere, inside),
+        out_specs=(anywhere, anywhere, inside),
         scratch_shapes=[
             vmem((nc, chunks, frames, coils, chunk, width), BF),
             vmem((nc, chunks, coils, chunk, width), BF),
@@ -391,19 +405,19 @@
             vmem((nf, frames, rows, width), BF),
             vmem((nc, nf, frames, rows, width), BF),
             vmem((frames, chunk, width), F32),
-            vmem((deep, long), BF),
-            vmem((deep, long), BF),
+            vmem((deep, 2 * long), BF),
             vmem((chunks, frames, chunk, width), F32),
             vmem((chunks, frames, chunk, width), F32),
             vmem((chunks, frames, chunk, width), F32),
             vmem((nf, frames, rows, width), BF),
             vmem((nf, frames, rows, width), BF),
             vmem((long, width), F32),
-            vmem((rows, rank, width), F32),
+            vmem((2 * long, width), BF),
             vmem((nf, frames, LANES), F32),
             vmem((nc, nf, frames, LANES), F32),
             dma((nc, chunks)),
             dma((nc, chunks)),
+            dma,
             dma,
             dma,
             dma,
@@ -421,6 +435,16 @@
             transcendentals=0,
         ),
     )(spatial, temporal, kspace, sampled, sensitivity, jnp.asarray(dft_block(width // 2)))
+    return pl.pallas_call(
+        factor_kernel,
+        out_shape=(
+            jax.ShapeDtypeStruct(spatial.shape, F32),
+            jax.ShapeDtypeStruct(temporal.shape, F32),
+        ),
+        in_specs=[inside] * 3,
+        out_specs=(inside, inside),
+        compiler_params=pltpu.CompilerParams(vmem_limit_bytes=24 * 1024 * 1024),
+    )(turn, grad_rows, temporal_sum)
 
 
 def solution(mesh):

time: 42.7 us -> 43.4 us (1.016)
  Pallas kernels: 38.4 us -> 39.8 us
  local copies, waits for them, and re-layouts: 3.53 us -> 2.74 us
    pallas_call x0 -> x1, Pallas kernels: none -> 1.41 us  [on_device(): pl.pallas_call(factor_kernel, out_shape=(jax.ShapeDtypeStruct(spatial.sha...]
    unnamed x2 -> x6, local copies, waits for them, and re-layouts: 3.53 us -> 2.74 us
where the time goes in v3:
time: 43.4 us; the launch traced here: 43.2 us
  Pallas kernels  39.8 us (92%)
  local copies, waits for them, and re-layouts  2.74 us (6%)
  between operations  0.65 us (1%)
    pallas_call x1, Pallas kernels, on_device(): pl.pallas_call(functools.partial(kernel, dims), out_shape=(jax.ShapeDtype...  38.4 us
    unnamed x6, local copies, waits for them, and re-layouts  2.74 us
    pallas_call x1, Pallas kernels, on_device(): pl.pallas_call(factor_kernel, out_shape=(jax.ShapeDtypeStruct(spatial.sha...  1.41 us

profile of v3, /device:TPU:0, one launch (start us, length us, event | category | flops | bytes accessed | tf_op | source)
XLA Modules:
  0.0 43.2 jit_solution(16129662540106674194)
XLA Ops:
  0.6 38.4 %shard_map.77 = (bf16[512,512]{1,0:T(8,128)(2,1)}, bf16[512,512]{1,0:T(8,128)(2,1)}, f32[2,64]{1,0:T(2,128)}) custom-call(bf16[16,32,512]{2,1,0:T(8,128)(2,1)} %spatial_hbm.1, bf16[2,64]{1,0:T(2,128)(2,1)} %temporal_ref.1, bf16[2,16,256,512]{3,2,1,0:T(8,128)(2,1)} %kspace_hbm.1, s32[2,256]{1,0:T(2,128)} %sampled_ref.1, bf16[16,256,512]{2,1,0:T(8,128)(2,1)} %sens_hbm.1, ...), custom_call_target="tpu_custom_call" | custom-call | flops 8589934592 | bytes 14155776 | tf_op jit(solution)/shard_map/pallas_call | solution.py:388
  39.0 0.0 copy-start
  39.0 1.0 %copy-done = bf16[512,512]{1,0:T(8,128)(2,1)S(1)} copy-done((bf16[512,512]{1,0:T(8,128)(2,1)S(1)}, bf16[512,512]{1,0:T(8,128)(2,1)}, u32[]{:S(2)}) %copy-start) | copy-done | bytes 524312
  40.0 0.0 copy-start.1
  40.0 1.0 %copy-done.1 = bf16[512,512]{1,0:T(8,128)(2,1)S(1)} copy-done((bf16[512,512]{1,0:T(8,128)(2,1)S(1)}, bf16[512,512]{1,0:T(8,128)(2,1)}, u32[]{:S(2)}) %copy-start.1) | copy-done | bytes 524312
  41.1 0.0 copy-start.2
  41.1 0.7 %copy-done.2 = f32[2,64]{1,0:T(2,128)S(1)} copy-done((f32[2,64]{1,0:T(2,128)S(1)}, f32[2,64]{1,0:T(2,128)}, u32[]{:S(2)}) %copy-start.2) | copy-done | bytes 536
  41.7 1.4 %shard_map.78 = (f32[16,32,512]{2,1,0:T(8,128)}, f32[2,64]{1,0:T(2,128)}) custom-call(bf16[512,512]{1,0:T(8,128)(2,1)S(1)} %copy-done, bf16[512,512]{1,0:T(8,128)(2,1)S(1)} %copy-done.1, f32[2,64]{1,0:T(2,128)S(1)} %copy-done.2), custom_call_target="tpu_custom_call" | custom-call | tf_op jit(solution)/shard_map/pallas_call | solution.py:438
Async XLA Ops:
  39.0 1.0 %copy-start = (bf16[512,512]{1,0:T(8,128)(2,1)S(1)}, bf16[512,512]{1,0:T(8,128)(2,1)}, u32[]{:S(2)}) copy-start(bf16[512,512]{1,0:T(8,128)(2,1)} %get-tuple-element.5.turn_ref) | copy-start | bytes 1572868
  40.0 1.0 %copy-start.1 = (bf16[512,512]{1,0:T(8,128)(2,1)S(1)}, bf16[512,512]{1,0:T(8,128)(2,1)}, u32[]{:S(2)}) copy-start(bf16[512,512]{1,0:T(8,128)(2,1)} %get-tuple-element.6.grad_ref) | copy-start | bytes 1572868
  41.1 0.7 %copy-start.2 = (f32[2,64]{1,0:T(2,128)S(1)}, f32[2,64]{1,0:T(2,128)}, u32[]{:S(2)}) copy-start(f32[2,64]{1,0:T(2,128)} %get-tuple-element.7.tsum_ref) | copy-start | bytes 1540

commit v4 on v3

--- a/solution.py
+++ b/solution.py
@@ -15,6 +15,7 @@
 MESH = pl.DeviceIdType.MESH
 ROW_TILE = 16
 AHEAD = 3
+LIMIT = 61 * 1024 * 1024
 LANES = 128
 
 
@@ -36,14 +37,17 @@
     return lax.dot_general(a, b, (((1,), (1,)), ((), ())), preferred_element_type=F32)
 
 
-def xor(a, b, count):
-    if count & (count - 1):
-        return lax.rem(a + b, count)
-    total, bit = 0, 1
-    while bit < count:
-        total = total + bit * lax.rem(a // bit + b // bit, 2)
-        bit *= 2
-    return total
+def ring(a, b, count):
+    total = a + b
+    return jnp.where(total >= count, total - count, total)
+
+
+def quotient(values, n):
+    return values >> (n.bit_length() - 1) if n & (n - 1) == 0 else values // n
+
+
+def remainder(values, n):
+    return values & (n - 1) if n & (n - 1) == 0 else lax.rem(values, n)
 
 
 def iota(shape, dim):
@@ -70,16 +74,10 @@
     total_frames = nf * frames
     f, c = lax.axis_index("frame"), lax.axis_index("coil")
     other = nc - 1 - c
-    mine = f // pieces
-
-    def order(step):
-        if chunks < 3:
-            return step
-        later = (step + chunks - 1) // chunks
-        return (lax.rem(step, chunks - 1) + 1) * later
+    mine = f if pieces == 1 else f // pieces
 
     def chunk_at(step):
-        return xor(mine, order(step), chunks)
+        return ring(mine, step, chunks)
 
     def remote(src, dst, ssem, rsem, frame, coil):
         return pltpu.make_async_remote_copy(
@@ -112,7 +110,7 @@
             if shift or coil:
                 pl.semaphore_signal(
                     barrier, inc=1,
-                    device_id={"frame": xor(f, shift, nf), "coil": lax.rem(c + coil, nc)},
+                    device_id={"frame": ring(f, shift, nf), "coil": (other if coil else c)},
                     device_id_type=MESH,
                 )
 
@@ -132,7 +130,7 @@
 
     pl.semaphore_wait(barrier, nf * nc - 1)
     for shift in range(1, nf):
-        to = xor(f, shift, nf)
+        to = ring(f, shift, nf)
         remote(tslot.at[f], tslot.at[f], t_ssem.at[to], t_rsem.at[f], to, c).start()
 
     block_copy.wait()
@@ -149,19 +147,19 @@
 
     spat_copy.wait()
     for shift in range(1, nf):
-        source = xor(f, shift, nf)
+        source = ring(f, shift, nf)
         remote(
             tslot.at[source], tslot.at[source], t_ssem.at[source], t_rsem.at[source], source, c
         ).wait_recv()
     for source in range(nf):
         tall[source * frames : (source + 1) * frames] = tslot[source]
     long, deep = total_frames * rows, rows * rank
-    repeat = one_hot(iota((long, total_frames), 0) // rows == iota((long, total_frames), 1))
+    repeat = one_hot(quotient(iota((long, total_frames), 0), rows) == iota((long, total_frames), 1))
     repeated = mm(repeat, tall[...].astype(BF)).astype(BF)
     lane, column = iota((LANES, deep), 0), iota((LANES, deep), 1)
-    same_row = lax.rem(iota((long, deep), 0), rows) == iota((long, deep), 1) // rank
-    spread_real = one_hot(lane == lax.rem(column, rank))
-    spread_imag = one_hot(lane == lax.rem(column, rank) + rank)
+    same_row = remainder(iota((long, deep), 0), rows) == quotient(iota((long, deep), 1), rank)
+    spread_real = one_hot(lane == remainder(column, rank))
+    spread_imag = one_hot(lane == remainder(column, rank) + rank)
     a_real = jnp.where(same_row, mm(repeated, spread_real), 0.0).astype(BF)
     a_imag = jnp.where(same_row, mm(repeated, spread_imag), 0.0).astype(BF)
     factors = spat[...].reshape(deep, width)
@@ -175,8 +173,7 @@
             img_send[to, t] = image[at : at + rows].astype(BF)
     img_recv[0, f] = img_send[f]
     for shift in range(1, nf):
-        shift = shift if nf < 3 else shift % (nf - 1) + 1
-        to = xor(f, shift, nf)
+        to = ring(f, shift, nf)
         remote(
             img_send.at[to], img_recv.at[0, f], i_ssem.at[to], i_rsem.at[f], to, c
         ).start()
@@ -185,9 +182,9 @@
         fetch(step)
 
     row, lane = iota((deep, LANES), 0), iota((deep, LANES), 1)
-    same_column = iota((deep, long), 0) // rank == lax.rem(iota((deep, long), 1), rows)
-    from_real = one_hot(lane == lax.rem(row, rank))
-    from_imag = one_hot(lane == lax.rem(row, rank) + rank)
+    same_column = quotient(iota((deep, long), 0), rank) == remainder(iota((deep, long), 1), rows)
+    from_real = one_hot(lane == remainder(row, rank))
+    from_imag = one_hot(lane == remainder(row, rank) + rank)
     turn[:, :long] = jnp.where(same_column, mm_nt(from_real, repeated), 0.0).astype(BF)
     turn[:, long:] = jnp.where(same_column, mm_nt(from_imag, repeated), 0.0).astype(BF)
     turn_copy = pltpu.make_async_copy(turn, turn_hbm, turn_sem)
@@ -303,7 +300,7 @@
         )
 
     for shift in range(1, nf):
-        gradient_copy(xor(f, shift, nf)).wait_recv()
+        gradient_copy(ring(f, shift, nf)).wait_recv()
     for source in range(nf):
         for t in range(frames):
             at = (source * frames + t) * rows
@@ -319,11 +316,11 @@
     pooled = jnp.zeros((long, LANES), F32)
     for values, shift in ((grad, 0), (turned, rank)):
         products = jnp.where(same_row, mm_nt(values, factors), 0.0)
-        fold = one_hot(lax.rem(fold_row, rank) + shift == fold_lane)
+        fold = one_hot(remainder(fold_row, rank) + shift == fold_lane)
         high = products.astype(BF)
         low = (products - high.astype(F32)).astype(BF)
         pooled = pooled + mm(high, fold) + mm(low, fold)
-    gather = one_hot(iota((total_frames, long), 0) == iota((total_frames, long), 1) // rows)
+    gather = one_hot(iota((total_frames, long), 0) == quotient(iota((total_frames, long), 1), rows))
     high = pooled.astype(BF)
     low = (pooled - high.astype(F32)).astype(BF)
     temporal_part = mm(gather, high) + mm(gather, low)
@@ -333,7 +330,7 @@
     for shift in range(nf):
         for coil in range(nc):
             if shift or coil:
-                to, at = xor(f, shift, nf), lax.rem(c + coil, nc)
+                to, at = ring(f, shift, nf), (other if coil else c)
                 remote(
                     tg_send.at[to], tg_recv.at[c, f], tg_ssem.at[at, to], tg_rsem.at[c, f], to, at
                 ).start()
@@ -341,7 +338,7 @@
     for shift in range(nf):
         for coil in range(nc):
             if shift or coil:
-                to, at = xor(f, shift, nf), lax.rem(c + coil, nc)
+                to, at = ring(f, shift, nf), (other if coil else c)
                 remote(
                     tg_send.at[to], tg_recv.at[at, to], tg_ssem.at[at, to], tg_rsem.at[at, to],
                     to, at,
@@ -354,7 +351,7 @@
     tgrad_ref[...] = summed[:, : 2 * rank]
 
     for shift in range(nf):
-        to = xor(f, shift, nf)
+        to = ring(f, shift, nf)
         forward_copy(to).wait_send()
         if shift:
             remote(tslot.at[f], tslot.at[f], t_ssem.at[to], t_rsem.at[f], to, c).wait_send()
@@ -369,9 +366,19 @@
     grad_copy.wait()
 
 
-def factor_kernel(turn_ref, grad_ref, tsum_ref, out_ref, tgrad_ref):
-    out_ref[...] = mm(turn_ref[...], grad_ref[...]).reshape(out_ref.shape)
-    tgrad_ref[...] = tsum_ref[...]
+def factor_kernel(
+    turn_hbm, grad_hbm, tsum_hbm, out_ref, tgrad_ref, turn, grad_rows, turn_sem, grad_sem, tsum_sem
+):
+    copies = (
+        pltpu.make_async_copy(turn_hbm, turn, turn_sem),
+        pltpu.make_async_copy(grad_hbm, grad_rows, grad_sem),
+        pltpu.make_async_copy(tsum_hbm, tgrad_ref, tsum_sem),
+    )
+    for copy in copies:
+        copy.start()
+    for copy in copies:
+        copy.wait()
+    out_ref[...] = mm(turn[...], grad_rows[...]).reshape(out_ref.shape)
 
 
 def on_device(nf, nc, spatial, temporal, kspace, sampled, sensitivity):
@@ -427,7 +434,7 @@
         + [dma((nf,))] * 2
         + [dma((nc, nf))] * 2,
         compiler_params=pltpu.CompilerParams(
-            collective_id=0, has_side_effects=True, vmem_limit_bytes=56 * 1024 * 1024
+            collective_id=0, has_side_effects=True, vmem_limit_bytes=LIMIT
         ),
         cost_estimate=pl.CostEstimate(
             flops=8 * frames * coils * nc * chunks * chunk * width * width // 2,
@@ -441,9 +448,10 @@
             jax.ShapeDtypeStruct(spatial.shape, F32),
             jax.ShapeDtypeStruct(temporal.shape, F32),
         ),
-        in_specs=[inside] * 3,
+        in_specs=[anywhere] * 3,
         out_specs=(inside, inside),
-        compiler_params=pltpu.CompilerParams(vmem_limit_bytes=24 * 1024 * 1024),
+        scratch_shapes=[vmem(turn.shape, BF), vmem(grad_rows.shape, BF), dma, dma, dma],
+        compiler_params=pltpu.CompilerParams(vmem_limit_bytes=LIMIT),
     )(turn, grad_rows, temporal_sum)
 
 

time: 43.4 us -> 44.4 us (1.023)
  Pallas kernels: 39.8 us -> 43.6 us
  local copies, waits for them, and re-layouts: 2.74 us -> 0 us
    unnamed x6 -> x0, local copies, waits for them, and re-layouts: 2.74 us -> none
    pallas_call x1, Pallas kernels: 38.4 us -> 41 us  [on_device(): pl.pallas_call(functools.partial(kernel, dims), out_shape=(jax.ShapeDtype...]
    pallas_call x1, Pallas kernels: 1.41 us -> 2.64 us  [on_device(): pl.pallas_call(factor_kernel, out_shape=(jax.ShapeDtypeStruct(spatial.sha...]
where the time goes in v4:
time: 44.4 us; the launch traced here: 44.2 us
  Pallas kernels  43.6 us (98%)
  between operations  0.64 us (1%)
    pallas_call x1, Pallas kernels, on_device(): pl.pallas_call(functools.partial(kernel, dims), out_shape=(jax.ShapeDtype...  41 us
    pallas_call x1, Pallas kernels, on_device(): pl.pallas_call(factor_kernel, out_shape=(jax.ShapeDtypeStruct(spatial.sha...  2.64 us

profile of v4, /device:TPU:0, one launch (start us, length us, event | category | flops | bytes accessed | tf_op | source)
XLA Modules:
  0.0 44.2 jit_solution(413641301795480611)
XLA Ops:
  0.6 41.0 %shard_map.77 = (bf16[512,512]{1,0:T(8,128)(2,1)}, bf16[512,512]{1,0:T(8,128)(2,1)}, f32[2,64]{1,0:T(2,128)}) custom-call(bf16[16,32,512]{2,1,0:T(8,128)(2,1)} %spatial_hbm.1, bf16[2,64]{1,0:T(2,128)(2,1)} %temporal_ref.1, bf16[2,16,256,512]{3,2,1,0:T(8,128)(2,1)} %kspace_hbm.1, s32[2,256]{1,0:T(2,128)} %sampled_ref.1, bf16[16,256,512]{2,1,0:T(8,128)(2,1)} %sens_hbm.1, ...), custom_call_target="tpu_custom_call" | custom-call | flops 8589934592 | bytes 14155776 | tf_op jit(solution)/shard_map/pallas_call | solution.py:395
  41.6 2.6 %shard_map.78 = (f32[16,32,512]{2,1,0:T(8,128)}, f32[2,64]{1,0:T(2,128)}) custom-call(bf16[512,512]{1,0:T(8,128)(2,1)} %get-tuple-element.5.turn_hbm, bf16[512,512]{1,0:T(8,128)(2,1)} %get-tuple-element.6.grad_hbm, f32[2,64]{1,0:T(2,128)} %get-tuple-element.7.tsum_hbm), custom_call_target="tpu_custom_call" | custom-call | tf_op jit(solution)/shard_map/pallas_call | solution.py:445

commit v5 on v4

--- a/solution.py
+++ b/solution.py
@@ -37,9 +37,18 @@
     return lax.dot_general(a, b, (((1,), (1,)), ((), ())), preferred_element_type=F32)
 
 
-def ring(a, b, count):
-    total = a + b
-    return jnp.where(total >= count, total - count, total)
+def xor(a, b, count):
+    if count & (count - 1):
+        return lax.rem(a + b, count)
+    total, bit = 0, 1
+    while bit < count:
+        if isinstance(b, int):
+            digit = lax.rem(lax.div(a, bit), 2)
+            total = total + bit * ((1 - digit) if b & bit else digit)
+        else:
+            total = total + bit * lax.rem(lax.div(a, bit) + lax.div(b, bit), 2)
+        bit *= 2
+    return total
 
 
 def quotient(values, n):
@@ -76,8 +85,16 @@
     other = nc - 1 - c
     mine = f if pieces == 1 else f // pieces
 
+    def order(step):
+        if chunks < 3:
+            return step
+        if isinstance(step, int):
+            return step % (chunks - 1) + 1 if step else 0
+        later = lax.div(step + chunks - 1, chunks)
+        return (lax.rem(step, chunks - 1) + 1) * later
+
     def chunk_at(step):
-        return ring(mine, step, chunks)
+        return xor(mine, order(step), chunks)
 
     def remote(src, dst, ssem, rsem, frame, coil):
         return pltpu.make_async_remote_copy(
@@ -110,7 +127,7 @@
             if shift or coil:
                 pl.semaphore_signal(
                     barrier, inc=1,
-                    device_id={"frame": ring(f, shift, nf), "coil": (other if coil else c)},
+                    device_id={"frame": xor(f, shift, nf), "coil": (other if coil else c)},
                     device_id_type=MESH,
                 )
 
@@ -130,7 +147,7 @@
 
     pl.semaphore_wait(barrier, nf * nc - 1)
     for shift in range(1, nf):
-        to = ring(f, shift, nf)
+        to = xor(f, shift, nf)
         remote(tslot.at[f], tslot.at[f], t_ssem.at[to], t_rsem.at[f], to, c).start()
 
     block_copy.wait()
@@ -147,7 +164,7 @@
 
     spat_copy.wait()
     for shift in range(1, nf):
-        source = ring(f, shift, nf)
+        source = xor(f, shift, nf)
         remote(
             tslot.at[source], tslot.at[source], t_ssem.at[source], t_rsem.at[source], source, c
         ).wait_recv()
@@ -173,7 +190,8 @@
             img_send[to, t] = image[at : at + rows].astype(BF)
     img_recv[0, f] = img_send[f]
     for shift in range(1, nf):
-        to = ring(f, shift, nf)
+        shift = shift if nf < 3 else shift % (nf - 1) + 1
+        to = xor(f, shift, nf)
         remote(
             img_send.at[to], img_recv.at[0, f], i_ssem.at[to], i_rsem.at[f], to, c
         ).start()
@@ -209,17 +227,19 @@
 
     def gradient(step, part):
         where = chunk_at(step)
-        for i in range(pieces):
-            for t in range(frames):
-                img_f32[t, i * rows : (i + 1) * rows] = img_recv[
-                    part, where * pieces + i, t
-                ].astype(F32)
+        if pieces > 1:
+            for i in range(pieces):
+                for t in range(frames):
+                    img_f32[t, i * rows : (i + 1) * rows] = img_recv[
+                        part, where * pieces + i, t
+                    ].astype(F32)
         for copy in chunk_copies(step, part):
             copy.wait()
         sums = []
         for t in range(frames):
-            image_real, image_imag = img_f32[t, :, :half], img_f32[t, :, half:]
-            sens = sbuf[part, step].astype(F32)
+            image = img_recv[part, where, t] if pieces == 1 else img_f32[t].astype(BF)
+            image_real, image_imag = image[:, :half], image[:, half:]
+            sens = sbuf[part, step]
             sens_real, sens_imag = sens[..., :half], sens[..., half:]
             coil_image = jnp.concatenate(
                 [
@@ -227,12 +247,13 @@
                     sens_real * image_imag[None] + sens_imag * image_real[None],
                 ],
                 -1,
-            ).astype(BF)
+            )
             spectrum = mm(coil_image.reshape(coils * chunk, width), block[...])
             measured = kbuf[part, step, t].reshape(coils * chunk, width).astype(F32)
             misfit = (spectrum - measured).astype(BF)
             adjoint = mm(misfit, back[t]).reshape(coils, chunk, width)
             back_real, back_imag = adjoint[..., :half], adjoint[..., half:]
+            sens_real, sens_imag = sens_real.astype(F32), sens_imag.astype(F32)
             sums.append(
                 jnp.concatenate(
                     [
@@ -300,7 +321,7 @@
         )
 
     for shift in range(1, nf):
-        gradient_copy(ring(f, shift, nf)).wait_recv()
+        gradient_copy(xor(f, shift, nf)).wait_recv()
     for source in range(nf):
         for t in range(frames):
             at = (source * frames + t) * rows
@@ -330,7 +351,7 @@
     for shift in range(nf):
         for coil in range(nc):
             if shift or coil:
-                to, at = ring(f, shift, nf), (other if coil else c)
+                to, at = xor(f, shift, nf), (other if coil else c)
                 remote(
                     tg_send.at[to], tg_recv.at[c, f], tg_ssem.at[at, to], tg_rsem.at[c, f], to, at
                 ).start()
@@ -338,7 +359,7 @@
     for shift in range(nf):
         for coil in range(nc):
             if shift or coil:
-                to, at = ring(f, shift, nf), (other if coil else c)
+                to, at = xor(f, shift, nf), (other if coil else c)
                 remote(
                     tg_send.at[to], tg_recv.at[at, to], tg_ssem.at[at, to], tg_rsem.at[at, to],
                     to, at,
@@ -351,7 +372,7 @@
     tgrad_ref[...] = summed[:, : 2 * rank]
 
     for shift in range(nf):
-        to = ring(f, shift, nf)
+        to = xor(f, shift, nf)
         forward_copy(to).wait_send()
         if shift:
             remote(tslot.at[f], tslot.at[f], t_ssem.at[to], t_rsem.at[f], to, c).wait_send()

time: 44.4 us -> 41.6 us (0.937)
  Pallas kernels: 43.6 us -> 40.7 us
    pallas_call x1, Pallas kernels: 41 us -> 38.1 us  [on_device(): pl.pallas_call(functools.partial(kernel, dims), out_shape=(jax.ShapeDtype...]
where the time goes in v5:
time: 41.6 us; the launch traced here: 41.4 us
  Pallas kernels  40.7 us (98%)
  between operations  0.64 us (2%)
    pallas_call x1, Pallas kernels, on_device(): pl.pallas_call(functools.partial(kernel, dims), out_shape=(jax.ShapeDtype...  38.1 us
    pallas_call x1, Pallas kernels, on_device(): pl.pallas_call(factor_kernel, out_shape=(jax.ShapeDtypeStruct(spatial.sha...  2.64 us

profile of v5, /device:TPU:0, one launch (start us, length us, event | category | flops | bytes accessed | tf_op | source)
XLA Modules:
  0.0 41.4 jit_solution(10329386285456701516)
XLA Ops:
  0.6 38.1 %shard_map.77 = (bf16[512,512]{1,0:T(8,128)(2,1)}, bf16[512,512]{1,0:T(8,128)(2,1)}, f32[2,64]{1,0:T(2,128)}) custom-call(bf16[16,32,512]{2,1,0:T(8,128)(2,1)} %spatial_hbm.1, bf16[2,64]{1,0:T(2,128)(2,1)} %temporal_ref.1, bf16[2,16,256,512]{3,2,1,0:T(8,128)(2,1)} %kspace_hbm.1, s32[2,256]{1,0:T(2,128)} %sampled_ref.1, bf16[16,256,512]{2,1,0:T(8,128)(2,1)} %sens_hbm.1, ...), custom_call_target="tpu_custom_call" | custom-call | flops 8589934592 | bytes 14155776 | tf_op jit(solution)/shard_map/pallas_call | solution.py:416
  38.7 2.6 %shard_map.78 = (f32[16,32,512]{2,1,0:T(8,128)}, f32[2,64]{1,0:T(2,128)}) custom-call(bf16[512,512]{1,0:T(8,128)(2,1)} %get-tuple-element.5.turn_hbm, bf16[512,512]{1,0:T(8,128)(2,1)} %get-tuple-element.6.grad_hbm, f32[2,64]{1,0:T(2,128)} %get-tuple-element.7.tsum_hbm), custom_call_target="tpu_custom_call" | custom-call | tf_op jit(solution)/shard_map/pallas_call | solution.py:466
